TPU v7x, 32 devices: a whole 2x2x4 slice. The times are simulated.
32 devices in a mesh: mp: 4 (over y, x), dp: 4 (over z), rep: 2 (over core).
Axes of the slice: x: 2, y: 2, z: 4, core: 2. Of those that a mesh axis runs over, the one named last changes fastest.
Arguments:
- states: bfloat16 [256, 32, 768], P(None, ('dp', 'rep')), may hold values from -26 to 26
- memory: bfloat16 [1024, 32, 768], P('mp', ('dp', 'rep')), may hold values from -6 to 6
- target_mask: int32 [32, 256], P(('dp', 'rep')), may hold values 0 or 1
- memory_length: int32 [32], P(('dp', 'rep')), may hold values from 512 to 1024, as said below
- norm_self: float32 [768], replicated, may hold values from 0.25 to 1.75
- self_query: bfloat16 [768, 768], P(None, 'mp'), may hold values from -0.02734375 to 0.02734375
- self_key: bfloat16 [768, 768], P(None, 'mp'), may hold values from -0.21875 to 0.21875
- self_value: bfloat16 [768, 768], P(None, 'mp'), may hold values from -0.21875 to 0.21875
- self_out: bfloat16 [768, 768], P('mp'), may hold values from -1.25 to 1.25
- bias_table: float32 [32, 12], P(None, 'mp'), may hold values from -4 to 4
- norm_cross: float32 [768], replicated, may hold values from 0.25 to 1.75
- cross_query: bfloat16 [768, 768], P(None, 'mp'), may hold values from -0.02734375 to 0.02734375
- cross_key: bfloat16 [768, 768], P(None, 'mp'), may hold values from -0.21875 to 0.21875
- cross_value: bfloat16 [768, 768], P(None, 'mp'), may hold values from -0.21875 to 0.21875
- cross_out: bfloat16 [768, 768], P('mp'), may hold values from -2.5 to 2.5
- norm_ffn: float32 [768], replicated, may hold values from 0.25 to 1.75
- ffn_gate: bfloat16 [768, 2048], P(None, 'mp'), may hold values from -0.21875 to 0.21875
- ffn_up: bfloat16 [768, 2048], P(None, 'mp'), may hold values from -0.21875 to 0.21875
- ffn_down: bfloat16 [2048, 768], P('mp'), may hold values from -0.125 to 0.125
- cotangent: bfloat16 [256, 32, 768], P('mp', ('dp', 'rep')), may hold values from -6 to 6
Outputs:
- block_out: bfloat16 [256, 32, 768], P('mp', ('dp', 'rep'))
- states_grad: float32 [256, 32, 768], P('mp', ('dp', 'rep'))
- memory_grad: float32 [1024, 32, 768], P('mp', ('dp', 'rep'))
- norm_self_grad: float32 [768], replicated
- self_query_grad: float32 [768, 768], P(None, 'mp')
- self_key_grad: float32 [768, 768], P(None, 'mp')
- self_value_grad: float32 [768, 768], P(None, 'mp')
- self_out_grad: float32 [768, 768], P('mp')
- bias_table_grad: float32 [32, 12], P(None, 'mp')
- norm_cross_grad: float32 [768], replicated
- cross_query_grad: float32 [768, 768], P(None, 'mp')
- cross_key_grad: float32 [768, 768], P(None, 'mp')
- cross_value_grad: float32 [768, 768], P(None, 'mp')
- cross_out_grad: float32 [768, 768], P('mp')
- norm_ffn_grad: float32 [768], replicated
- ffn_gate_grad: float32 [768, 2048], P(None, 'mp')
- ffn_up_grad: float32 [768, 2048], P(None, 'mp')
- ffn_down_grad: float32 [2048, 768], P('mp')
Inputs may be any that keep to these rules, and one draw needn't show every extreme that they name: `memory_length`: each sequence has 512 or 1024 live memory slots; among the sequences of one index of dp and rep at least one has 1024.
All inputs are finite; a program needn't handle non-finite values. No bound on the sum of `target_mask` on one device may be relied on, other than what follows from the above.
Results may differ from a plain program's by a relative error of at most 0.022.
Values may be sent and summed in bfloat16 or wider, within the bound.
A program may use at most 192 MiB of HBM per device.

v0:
```python
import math

import jax
import jax.numpy as jnp
from jax import lax
from jax.sharding import PartitionSpec as P

eps = 1e-06
bucket_edges = [math.ceil(16 * 8 ** (level / 16)) for level in range(1, 16)]


def bucket_of(offset):
    edge_list = jnp.array(bucket_edges, dtype=jnp.int32)
    passed = jnp.sum((offset[..., None] >= edge_list).astype(jnp.int32), axis=-1)
    return jnp.minimum(offset, 16) + passed


def normalize(values, gain):
    return values * lax.rsqrt(jnp.mean(values * values, axis=-1, keepdims=True) + eps) * gain


def norm_back(values, gain, incoming):
    unused, pullback = jax.vjp(lambda argument: normalize(argument, gain), values)
    return pullback(incoming)[0]


def gain_part(values, incoming):
    inverse_rms = lax.rsqrt(jnp.mean(values * values, axis=-1, keepdims=True) + eps)
    return jnp.sum(incoming * values * inverse_rms, axis=(0, 1))


def project(values, weight):
    return jnp.einsum("tbd,de->tbe", values, weight, preferred_element_type=jnp.float32)


def back_project(gradient, weight):
    return jnp.einsum("tbe,de->tbd", gradient, weight, preferred_element_type=jnp.float32)


def weight_grad(values, gradient):
    return jnp.einsum("tbd,tbe->de", values, gradient, preferred_element_type=jnp.float32)


def split_heads(values, head_count):
    return values.reshape(
        values.shape[0], values.shape[1], head_count, values.shape[2] // head_count
    )


def scores_of(query_rows, key_rows, score_bias, allowed, head_count):
    attention_scores = (
        jnp.einsum(
            "tbhd,mbhd->bhtm",
            split_heads(query_rows, head_count),
            split_heads(key_rows, head_count),
            preferred_element_type=jnp.float32,
        )
        + score_bias
    )
    return jnp.where(allowed, attention_scores, -1e30)


def attend(query_rows, key_rows, value_rows, score_bias, allowed, head_count):
    attention_scores = scores_of(query_rows, key_rows, score_bias, allowed, head_count)
    row_max = jnp.max(attention_scores, axis=-1, keepdims=True)
    weights = jnp.exp(attention_scores - row_max)
    row_total = jnp.sum(weights, axis=-1, keepdims=True)
    attention_mix = (weights / row_total).astype(jnp.bfloat16)
    combined_heads = jnp.einsum(
        "bhtm,mbhd->tbhd",
        attention_mix,
        split_heads(value_rows, head_count),
        preferred_element_type=jnp.float32,
    )
    return (
        combined_heads.reshape(query_rows.shape).astype(jnp.bfloat16),
        row_max + jnp.log(row_total),
    )


def attend_back(
    query_rows, key_rows, value_rows, score_bias, allowed, head_count, logsum, incoming
):
    attention_scores = scores_of(query_rows, key_rows, score_bias, allowed, head_count)
    attention_mix = jnp.exp(attention_scores - logsum)
    upstream = split_heads(incoming, head_count)
    value_grad = jnp.einsum(
        "bhtm,tbhd->mbhd",
        attention_mix.astype(jnp.bfloat16),
        upstream,
        preferred_element_type=jnp.float32,
    )
    weight_gradient = jnp.einsum(
        "tbhd,mbhd->bhtm",
        upstream,
        split_heads(value_rows, head_count),
        preferred_element_type=jnp.float32,
    )
    score_grad = attention_mix * (
        weight_gradient - jnp.sum(attention_mix * weight_gradient, axis=-1, keepdims=True)
    )
    score_grad = score_grad.astype(jnp.bfloat16)
    query_grad = jnp.einsum(
        "bhtm,mbhd->tbhd",
        score_grad,
        split_heads(key_rows, head_count),
        preferred_element_type=jnp.float32,
    )
    key_grad = jnp.einsum(
        "bhtm,tbhd->mbhd",
        score_grad,
        split_heads(query_rows, head_count),
        preferred_element_type=jnp.float32,
    )
    return (
        query_grad.reshape(query_rows.shape).astype(jnp.bfloat16),
        key_grad.reshape(key_rows.shape).astype(jnp.bfloat16),
        value_grad.reshape(value_rows.shape).astype(jnp.bfloat16),
        score_grad,
    )


def whole_add(residual, partial_value):
    return residual + lax.psum(partial_value, "mp")


def grad_whole(partial_value):
    return lax.psum(partial_value, "mp")


def per_device(
    states,
    memory,
    target_mask,
    memory_length,
    norm_self,
    self_query,
    self_key,
    self_value,
    self_out,
    bias_table,
    norm_cross,
    cross_query,
    cross_key,
    cross_value,
    cross_out,
    norm_ffn,
    ffn_gate,
    ffn_up,
    ffn_down,
    cotangent,
):
    target_len = states.shape[0]
    model_ways = lax.axis_size("mp")
    own_count = target_len // model_ways
    own_start = lax.axis_index("mp") * own_count
    head_count = bias_table.shape[1]
    memory_slots = memory.shape[0] * model_ways
    positions = jnp.arange(target_len, dtype=jnp.int32)
    distance = jnp.maximum(positions[:, None] - positions[None, :], 0)
    onehot = (
        bucket_of(distance)[:, :, None] == jnp.arange(bias_table.shape[0], dtype=jnp.int32)
    ).astype(jnp.float32)
    relative_position_bias = jnp.einsum(
        "ijk,kh->hij", onehot, bias_table, precision=lax.Precision.HIGHEST
    )[None]
    diagonal = positions[:, None] == positions[None, :]
    self_ok = (
        (positions[:, None] >= positions[None, :])[None]
        & ((target_mask[:, None, :] != 0) | diagonal[None])
    )[:, None]
    cross_ok = (jnp.arange(memory_slots, dtype=jnp.int32)[None, :] < memory_length[:, None])[
        :, None, None, :
    ]
    resident = states.astype(jnp.float32)
    own_rows = lax.dynamic_slice_in_dim(resident, own_start, own_count, 0)
    normed_self = normalize(resident, norm_self).astype(jnp.bfloat16)
    query_self = project(normed_self, self_query).astype(jnp.bfloat16)
    key_self = project(normed_self, self_key).astype(jnp.bfloat16)
    value_self = project(normed_self, self_value).astype(jnp.bfloat16)
    attended_self, logsum_self = attend(
        query_self, key_self, value_self, relative_position_bias, self_ok, head_count
    )
    branch_self = project(attended_self, self_out)
    memory_full = lax.all_gather(memory, "mp", axis=0, tiled=True)
    key_cross = project(memory_full, cross_key).astype(jnp.bfloat16)
    value_cross = project(memory_full, cross_value).astype(jnp.bfloat16)
    first_sum = whole_add(resident, branch_self)
    normed_cross = normalize(first_sum, norm_cross).astype(jnp.bfloat16)
    query_cross = project(normed_cross, cross_query).astype(jnp.bfloat16)
    attended_cross, logsum_cross = attend(
        query_cross, key_cross, value_cross, 0.0, cross_ok, head_count
    )
    branch_cross = project(attended_cross, cross_out)
    second_sum = whole_add(first_sum, branch_cross)
    normed_ffn = normalize(second_sum, norm_ffn).astype(jnp.bfloat16)
    second_own = lax.dynamic_slice_in_dim(second_sum, own_start, own_count, 0)
    gate_part = project(normed_ffn, ffn_gate)
    up_part = project(normed_ffn, ffn_up)
    hidden = (jax.nn.gelu(gate_part, approximate=True) * up_part).astype(jnp.bfloat16)
    branch_ffn = project(hidden, ffn_down)
    block_out = (
        second_own
        + lax.psum_scatter(
            branch_ffn.astype(jnp.bfloat16), "mp", scatter_dimension=0, tiled=True
        ).astype(jnp.float32)
    ).astype(jnp.bfloat16)
    upstream = lax.all_gather(cotangent, "mp", axis=0, tiled=True)
    ffn_down_grad = weight_grad(hidden, upstream)
    hidden_grad = back_project(upstream, ffn_down)
    unused, pullback = jax.vjp(
        lambda gate_in, up_in: jax.nn.gelu(gate_in, approximate=True) * up_in, gate_part, up_part
    )
    gate_grad, up_grad = pullback(hidden_grad)
    gate_grad = gate_grad.astype(jnp.bfloat16)
    up_grad = up_grad.astype(jnp.bfloat16)
    ffn_gate_grad = weight_grad(normed_ffn, gate_grad)
    ffn_up_grad = weight_grad(normed_ffn, up_grad)
    normed_grad = back_project(gate_grad, ffn_gate) + back_project(up_grad, ffn_up)
    normed_grad = grad_whole(normed_grad)
    second_grad = upstream.astype(jnp.float32) + norm_back(second_sum, norm_ffn, normed_grad)
    ffn_gain = gain_part(second_own, lax.dynamic_slice_in_dim(normed_grad, own_start, own_count, 0))
    cross_upstream = second_grad.astype(jnp.bfloat16)
    cross_out_grad = weight_grad(attended_cross, cross_upstream)
    attended_grad = back_project(cross_upstream, cross_out).astype(jnp.bfloat16)
    query_grad, key_grad, value_grad, unused_scores = attend_back(
        query_cross, key_cross, value_cross, 0.0, cross_ok, head_count, logsum_cross, attended_grad
    )
    cross_query_grad = weight_grad(normed_cross, query_grad)
    cross_key_grad = weight_grad(memory_full, key_grad)
    cross_value_grad = weight_grad(memory_full, value_grad)
    key_rows = key_grad
    value_rows = value_grad
    memory_grad = lax.psum_scatter(
        (back_project(key_rows, cross_key) + back_project(value_rows, cross_value)).astype(
            jnp.bfloat16
        ),
        "mp",
        scatter_dimension=0,
        tiled=True,
    ).astype(jnp.float32)
    normed_grad = back_project(query_grad, cross_query)
    normed_grad = grad_whole(normed_grad)
    first_grad = second_grad + norm_back(first_sum, norm_cross, normed_grad)
    cross_gain = gain_part(
        lax.dynamic_slice_in_dim(first_sum, own_start, own_count, 0),
        lax.dynamic_slice_in_dim(normed_grad, own_start, own_count, 0),
    )
    self_upstream = first_grad.astype(jnp.bfloat16)
    first_grad_own = lax.dynamic_slice_in_dim(first_grad, own_start, own_count, 0)
    self_out_grad = weight_grad(attended_self, self_upstream)
    attended_grad = back_project(self_upstream, self_out).astype(jnp.bfloat16)
    query_grad, key_grad, value_grad, score_grad = attend_back(
        query_self,
        key_self,
        value_self,
        relative_position_bias,
        self_ok,
        head_count,
        logsum_self,
        attended_grad,
    )
    bias_table_grad = jnp.einsum(
        "hij,ijk->kh",
        jnp.sum(score_grad.astype(jnp.float32), axis=0),
        onehot,
        precision=lax.Precision.HIGHEST,
    )
    self_query_grad = weight_grad(normed_self, query_grad)
    self_key_grad = weight_grad(normed_self, key_grad)
    self_value_grad = weight_grad(normed_self, value_grad)
    normed_grad = (
        back_project(query_grad, self_query)
        + back_project(key_grad, self_key)
        + back_project(value_grad, self_value)
    )
    normed_grad = lax.psum_scatter(
        normed_grad.astype(jnp.bfloat16), "mp", scatter_dimension=0, tiled=True
    ).astype(jnp.float32)
    states_grad = first_grad_own + norm_back(own_rows, norm_self, normed_grad)
    self_gain = gain_part(own_rows, normed_grad)
    summed = lax.psum(
        (
            self_query_grad,
            self_key_grad,
            self_value_grad,
            self_out_grad,
            bias_table_grad,
            cross_query_grad,
            cross_key_grad,
            cross_value_grad,
            cross_out_grad,
            ffn_gate_grad,
            ffn_up_grad,
            ffn_down_grad,
        ),
        ("dp", "rep"),
    )
    gains = lax.psum((self_gain, cross_gain, ffn_gain), ("mp", "dp", "rep"))
    return (
        block_out,
        states_grad,
        memory_grad,
        gains[0],
        summed[0],
        summed[1],
        summed[2],
        summed[3],
        summed[4],
        gains[1],
        summed[5],
        summed[6],
        summed[7],
        summed[8],
        gains[2],
        summed[9],
        summed[10],
        summed[11],
    )


def solution(mesh):
    in_specs = (
        P(None, ("dp", "rep"), None),
        P("mp", ("dp", "rep"), None),
        P(("dp", "rep"), None),
        P(("dp", "rep")),
        P(),
        P(None, "mp"),
        P(None, "mp"),
        P(None, "mp"),
        P("mp", None),
        P(None, "mp"),
        P(),
        P(None, "mp"),
        P(None, "mp"),
        P(None, "mp"),
        P("mp", None),
        P(),
        P(None, "mp"),
        P(None, "mp"),
        P("mp", None),
        P("mp", ("dp", "rep"), None),
    )
    out_specs = (
        P("mp", ("dp", "rep"), None),
        P("mp", ("dp", "rep"), None),
        P("mp", ("dp", "rep"), None),
        P(),
        P(None, "mp"),
        P(None, "mp"),
        P(None, "mp"),
        P("mp", None),
        P(None, "mp"),
        P(),
        P(None, "mp"),
        P(None, "mp"),
        P(None, "mp"),
        P("mp", None),
        P(),
        P(None, "mp"),
        P(None, "mp"),
        P("mp", None),
    )
    return jax.shard_map(
        per_device, mesh=mesh, in_specs=in_specs, out_specs=out_specs, check_vma=False
    )
```

profile of v0, /device:TPU:0, one launch (start us, length us, event | category | flops | bytes accessed | tf_op | source)
XLA Modules:
  0.0 912.1 jit_solution(5840914356010735202)
XLA Ops:
  11.8 4.3 fusion.30
  25.6 2.7 copy.71
  28.8 86.9 %all-reduce.8.cloned.1.call-done = f32[256,4,768]{2,0,1:T(8,128)} async-done(((f32[256,4,768]{2,0,1:T(8,128)}), f32[256,4,768]{2,0,1:T(8,128)}) %all-reduce.8.cloned.1.call-update) | async-done | bytes 3145744 | tf_op jit(solution)/shard_map/psum | solution.py:124
  120.4 68.0 %all-gather.3.cloned.1.call-done = bf16[1024,4,768]{2,0,1:T(8,128)(2,1)} async-done(((bf16[256,4,768]{2,0,1:T(8,128)(2,1)}), bf16[1024,4,768]{2,0,1:T(8,128)(2,1)}) %all-gather.3.cloned.1.call-update) | async-done | bytes 6291472 | tf_op jit(solution)/shard_map/all_gather | solution.py:185
  188.4 5.1 convolution_convert_fusion.2
  195.5 2.9 fusion
  200.7 3.6 fusion.35
  209.0 85.0 %all-reduce.10.cloned.1.call-done = f32[256,4,768]{2,0,1:T(8,128)} async-done(((f32[256,4,768]{2,0,1:T(8,128)}), f32[256,4,768]{2,0,1:T(8,128)}) %all-reduce.10.cloned.1.call-update) | async-done | bytes 3145744 | tf_op jit(solution)/shard_map/psum | solution.py:124
  294.0 3.3 multiply_reduce_fusion.4
  303.7 23.7 %all-gather.5.cloned.1.call-done = bf16[256,4,768]{2,0,1:T(8,128)(2,1)} async-done(((bf16[64,4,768]{2,0,1:T(8,128)(2,1)}), bf16[256,4,768]{2,0,1:T(8,128)(2,1)}) %all-gather.5.cloned.1.call-update) | async-done | bytes 1572880 | tf_op jit(solution)/shard_map/all_gather | solution.py:208
  327.3 5.4 multiply_convert_fusion.5
  338.7 86.0 %all-reduce.12.cloned.1.call-done = f32[256,4,768]{2,0,1:T(8,128)} async-done(((f32[256,4,768]{2,0,1:T(8,128)}), f32[256,4,768]{2,0,1:T(8,128)}) %all-reduce.12.cloned.1.call-update) | async-done | bytes 3145744 | tf_op jit(solution)/shard_map/psum | solution.py:128
  424.8 3.4 multiply_reduce_fusion.3
  434.4 10.8 %multiply_reduce_fusion = (f32[4,3,256]{2,1,0:T(4,128)S(1)}, f32[4,3,256,1024]{3,2,1,0:T(8,128)}) fusion(f32[4,3,256,1024]{3,2,1,0:T(8,128)} %copy-done.2, f32[4,3,256]{2,1,0:T(4,128)S(1)} %copy-done.70, pred[4,1024]{1,0:T(4,128)(4,1)S(1)} %iota_compare_fusion.9, bf16[256,4,3,64]{0,3,2,1:T(8,128)(2,1)S(1)} %bitcast.209, ...), kind=kOutput, calls=%fused_computation.2 | convolution fusion | flops 415233024 | bytes 27160576 | tf_op jit(solution)/shard_map/tbhd,mbhd->bhtm/dot_general | solution.py:93
  445.2 6.7 multiply_convert_fusion
  458.2 3.3 convolution_convert_fusion
  461.9 82.3 %all-reduce.14.cloned.1.call-done = f32[256,4,768]{2,0,1:T(8,128)} async-done(((f32[256,4,768]{2,0,1:T(8,128)}), f32[256,4,768]{2,0,1:T(8,128)}) %all-reduce.14.cloned.1.call-update) | async-done | bytes 3145744 | tf_op jit(solution)/shard_map/psum | solution.py:128
  544.2 3.4 multiply_reduce_fusion.2
  547.9 5.0 fusion.13
  563.5 4.2 convolution_convert_fusion.1
  567.8 3.5 fusion.59
  571.4 3.5 fusion.23
  574.9 6.0 add_convert_fusion
  581.2 4.0 convolution_bitcast_fusion.2
  592.5 5.3 convolution_bitcast_fusion.10
  597.8 5.3 convolution_bitcast_fusion.9
  616.9 4.2 fusion.36
  621.1 16.9 %psum.142 = f32[32,3]{0,1:T(4,128)} all-reduce(f32[32,3]{0,1:T(4,128)S(1)} %fusion.36), channel_id=1, replica_groups=mesh['mp'=4,'dp'=4,'rep'=2] {'dp','rep'}, use_global_device_ids=true, to_apply=%region_28.29 | all-reduce | flops 96 | bytes 768 | tf_op jit(solution)/shard_map/psum | solution.py:282
  644.3 37.5 %all-reduce = (f32[768]{0:T(1024)}, f32[768]{0:T(1024)}, f32[768]{0:T(1024)}) all-reduce(f32[768]{0:T(1024)S(1)} %get-tuple-element.72, f32[768]{0:T(1024)S(1)} %multiply_reduce_fusion.9, f32[768]{0:T(1024)S(1)} %get-tuple-element.97), channel_id=1, replica_groups=mesh['mp'=4,'dp'=4,'rep'=2] {'mp','dp','rep'}, use_global_device_ids=true, to_apply=%region_22.23 | all-reduce | flops 2304 | bytes 18432 | tf_op jit(solution)/shard_map/psum | solution.py:299
  681.8 6.1 reduce-scatter.8.cloned.1.call-done
  687.9 4.3 copy.82
  692.2 199.1 %all-reduce.16.cloned.1.call-done = (f32[768,192]{0,1:T(8,128)}, f32[768,192]{0,1:T(8,128)}, f32[768,192]{0,1:T(8,128)}, f32[192,768]{1,0:T(8,128)}, f32[768,192...) async-done(((f32[768,192]{0,1:T(8,128)}, ...) | async-done | bytes 9437200 | tf_op jit(solution)/shard_map/psum | solution.py:282
  (320 shorter events, 104.6 us)
Async XLA Ops:
  7.2 320.1 %copy-start = (bf16[512,768]{1,0:T(8,128)(2,1)S(1)}, bf16[512,768]{1,0:T(8,128)(2,1)}, u32[]{:S(2)}) copy-start(bf16[512,768]{1,0:T(8,128)(2,1)} %param.39) | copy-start | bytes 2359300
  7.2 108.4 %all-reduce.8.cloned.1.call-start = ((), (), s32[]{:S(2)}) async-start(), calls=%async_computation.3 | async-start | bytes 6291456 | tf_op jit(solution)/shard_map/psum | solution.py:124
  8.0 9.6 %copy-start.14 = (bf16[256,4,768]{2,1,0:T(4,128)(2,1)S(1)}, bf16[256,4,768]{2,1,0:T(4,128)(2,1)}, u32[]{:S(2)}) copy-start(bf16[256,4,768]{2,1,0:T(4,128)(2,1)} %param.21) | copy-start | bytes 4718596
  8.0 9.6 %copy-start.60 = (bf16[768,192]{0,1:T(8,128)(2,1)S(1)}, bf16[768,192]{0,1:T(8,128)(2,1)}, u32[]{:S(2)}) copy-start(bf16[768,192]{0,1:T(8,128)(2,1)} %param.28) | copy-start | bytes 884740
  8.0 9.6 %copy-start.92 = (f32[768]{0:T(1024)S(1)}, f32[768]{0:T(1024)}, u32[]{:S(2)}) copy-start(f32[768]{0:T(1024)} %param.25) | copy-start | bytes 9220
  9.9 9.4 %copy-start.95 = (f32[256,4]{0,1:T(4,128)}, f32[256,4]{0,1:T(4,128)S(1)}, u32[]{:S(2)}) copy-start(f32[256,4]{0,1:T(4,128)S(1)} %add_rsqrt_fusion) | copy-start | bytes 12292
  25.6 162.8 %all-gather.3.cloned.1.call-start = ((), (), s32[]{:S(2)}) async-start(), calls=%async_computation.4 | async-start | bytes 7864320 | tf_op jit(solution)/shard_map/all_gather | solution.py:185
  28.4 265.6 %all-reduce.10.cloned.1.call-start = ((), (), s32[]{:S(2)}) async-start(), calls=%async_computation.5 | async-start | bytes 6291456 | tf_op jit(solution)/shard_map/psum | solution.py:124
  28.8 90.9 %copy-start.42 = (bf16[768,192]{0,1:T(8,128)(2,1)S(1)}, bf16[768,192]{0,1:T(8,128)(2,1)}, u32[]{:S(2)}) copy-start(bf16[768,192]{0,1:T(8,128)(2,1)} %param.32) | copy-start | bytes 884740
  28.8 90.9 %copy-start.84 = (f32[768]{0:T(1024)S(1)}, f32[768]{0:T(1024)}, u32[]{:S(2)}) copy-start(f32[768]{0:T(1024)} %param.31) | copy-start | bytes 9220
  117.9 75.6 %copy-start.90 = (f32[256,4]{0,1:T(4,128)}, f32[256,4]{0,1:T(4,128)S(1)}, u32[]{:S(2)}) copy-start(f32[256,4]{0,1:T(4,128)S(1)} %get-tuple-element.92) | copy-start | bytes 12292
  118.0 75.5 %copy-start.85 = (f32[256,4]{0,1:T(4,128)}, f32[256,4]{0,1:T(4,128)S(1)}, u32[]{:S(2)}) copy-start(f32[256,4]{0,1:T(4,128)S(1)} %fusion.79) | copy-start | bytes 12292
  188.4 10.0 %slice-start.6 = ((s8[6291456]{0:T(1024)(128)(4,1)}), s8[4194304]{0:T(1024)(128)(4,1)S(1)}, s32[]{:S(2)}) async-start(s8[6291456]{0:T(1024)(128)(4,1)} %bitcast.213), calls=%async_computation.19 | async-start | bytes 8388608
  206.7 120.6 %all-gather.5.cloned.1.call-start = ((), (), s32[]{:S(2)}) async-start(), calls=%async_computation.7 | async-start | bytes 1966080 | tf_op jit(solution)/shard_map/all_gather | solution.py:208
  208.6 88.8 %copy-start.80 = (f32[768]{0:T(1024)S(1)}, f32[768]{0:T(1024)}, u32[]{:S(2)}) copy-start(f32[768]{0:T(1024)} %param.36) | copy-start | bytes 9220
  208.6 216.2 %all-reduce.12.cloned.1.call-start = ((), (), s32[]{:S(2)}) async-start(), calls=%async_computation.8 | async-start | bytes 6291456 | tf_op jit(solution)/shard_map/psum | solution.py:128
  337.4 206.8 %all-reduce.14.cloned.1.call-start = ((), (), s32[]{:S(2)}) async-start(), calls=%async_computation.9 | async-start | bytes 6291456 | tf_op jit(solution)/shard_map/psum | solution.py:128
  433.6 11.5 %copy-start.40 = (bf16[256,4,192]{0,2,1:T(8,128)(2,1)}, bf16[256,4,192]{0,2,1:T(8,128)(2,1)S(1)}, u32[]{:S(2)}) copy-start(bf16[256,4,192]{0,2,1:T(8,128)(2,1)S(1)} %convolution_convert_fusion.8) | copy-start | bytes 1179652
  433.6 11.5 %slice-start = ((s8[12582912]{0:T(1024)(128)(4,1)}), s8[4194304]{0:T(1024)(128)(4,1)S(1)}, s32[]{:S(2)}) async-start(s8[12582912]{0:T(1024)(128)(4,1)} %bitcast.177), calls=%async_computation.13 | async-start | bytes 8388608
  434.4 10.8 %slice-start.1 = ((s8[12582912]{0:T(1024)(128)(4,1)}), s8[4194304]{0:T(1024)(128)(4,1)S(1)}, s32[]{:S(2)}) async-start(s8[12582912]{0:T(1024)(128)(4,1)} %bitcast.177), calls=%async_computation.14 | async-start | bytes 8388608
  434.4 10.8 %slice-start.2 = ((s8[12582912]{0:T(1024)(128)(4,1)}), s8[4194304]{0:T(1024)(128)(4,1)S(1)}, s32[]{:S(2)}) async-start(s8[12582912]{0:T(1024)(128)(4,1)} %bitcast.177), calls=%async_computation.15 | async-start | bytes 8388608
  456.8 157.0 %reduce-scatter.4.cloned.1.call-start = ((), (), s32[]{:S(2)}) async-start(), calls=%async_computation.6 | async-start | bytes 1966080 | tf_op jit(solution)/shard_map/reduce_scatter | solution.py:204
  461.6 85.9 %copy-start.91 = (f32[256,4]{0,1:T(4,128)S(1)}, f32[256,4]{0,1:T(4,128)}, u32[]{:S(2)}) copy-start(f32[256,4]{0,1:T(4,128)} %copy-done.90) | copy-start | bytes 12292
  461.6 86.0 %copy-start.86 = (f32[256,4]{0,1:T(4,128)S(1)}, f32[256,4]{0,1:T(4,128)}, u32[]{:S(2)}) copy-start(f32[256,4]{0,1:T(4,128)} %copy-done.85) | copy-start | bytes 12292
  461.6 86.0 %copy-start.89 = (f32[256,4]{0,1:T(4,128)S(1)}, f32[256,4]{0,1:T(4,128)}, u32[]{:S(2)}) copy-start(f32[256,4]{0,1:T(4,128)} %copy-done.88) | copy-start | bytes 12292
  461.6 177.9 %reduce-scatter.6.cloned.1.call-start = ((), (), s32[]{:S(2)}) async-start(), calls=%async_computation.10 | async-start | bytes 1966080 | tf_op jit(solution)/shard_map/reduce_scatter | solution.py:277
  563.4 124.5 %reduce-scatter.8.cloned.1.call-start = ((), (), s32[]{:S(2)}) async-start(), calls=%async_computation.11 | async-start | bytes 7864320 | tf_op jit(solution)/shard_map/reduce_scatter | solution.py:234
  563.4 7.9 slice-start.3
  563.5 7.9 slice-start.4
  580.9 310.3 %all-reduce.16.cloned.1.call-start = ((), (), s32[]{:S(2)}) async-start(), calls=%async_computation.12 | async-start | bytes 18874368 | tf_op jit(solution)/shard_map/psum | solution.py:282
  891.2 6.8 copy-start.56
  891.2 7.6 copy-start.55
  (85 other events, 246.7 us)
Sparse Core Ops, SparseCore 0:
  25.7 89.8 all-reduce.7
  118.2 70.1 all-gather.2
  206.8 87.1 all-reduce.9
  296.3 30.9 all-gather.4
  337.5 87.1 all-reduce.11
  456.9 87.1 all-reduce.13
  547.7 30.9 reduce-scatter.3
  582.3 30.9 reduce-scatter.5
  616.2 71.6 reduce-scatter.7
  692.2 198.9 all-reduce.15
where the time goes:
time: 919 us; the launch traced here: 912 us
  waiting for transfers between devices  637 us (69%)
  matrix products  114 us (12%)
  blocking collectives  54.4 us (6%)
  other arithmetic  47.4 us (5%)
  local copies, waits for them, and re-layouts  41.5 us (5%)
  between operations  15.8 us (2%)
    psum x1, waiting for transfers between devices, per_device(): lax.psum((self_query_grad, self_key_grad, self_value_grad, self_out_grad,...  199 us
    psum x2, waiting for transfers between devices, whole_add(): return residual + lax.psum(partial_value, 'mp')  172 us
    psum x2, waiting for transfers between devices, grad_whole(): return lax.psum(partial_value, 'mp')  168 us
    all_gather x1, waiting for transfers between devices, per_device(): memory_full = lax.all_gather(memory, 'mp', axis=0, tiled=True)  68 us
    unnamed x230, local copies, waits for them, and re-layouts  39.6 us
    psum x1, blocking collectives, per_device(): gains = lax.psum((self_gain, cross_gain, ffn_gain), ('mp', 'dp', 'rep'))  37.5 us
    dot_general x11, matrix products, weight_grad(): jnp.einsum('tbd,tbe->de', values, gradient, preferred_element_type=jnp.fl...  27.7 us
    dot_general x11, matrix products, back_project(): jnp.einsum('tbe,de->tbd', gradient, weight, preferred_element_type=jnp.fl...  25.3 us
  transfers between devices with their start and end apart: 10, of which 8 were waited for; matrix products, arithmetic and copies ran while one was open for 11% of the time, Pallas kernels for 0%

commit v1 on v0

v1 whole, which is shorter than its diff:
```python
import math
import types

import jax
import jax.numpy as jnp
from jax import lax
from jax.experimental import pallas as pl
from jax.experimental.pallas import tpu as pltpu
from jax.sharding import PartitionSpec as P

eps = 1e-06
bucket_edges = [math.ceil(16 * 8 ** (level / 16)) for level in range(1, 16)]
BF = jnp.bfloat16
F32 = jnp.float32
NEG = -1e30
MESH = pl.DeviceIdType.MESH
WAYS = 4
CK, CV, SO, CQ, CO = range(5)


def bucket_of(offset):
    edge_list = jnp.array(bucket_edges, dtype=jnp.int32)
    passed = jnp.sum((offset[..., None] >= edge_list).astype(jnp.int32), axis=-1)
    return jnp.minimum(offset, 16) + passed


def dots(a, b, ca, cb):
    return lax.dot_general(a, b, (((ca,), (cb,)), ((), ())), preferred_element_type=F32)


def nn(a, b):
    return dots(a, b, 1, 0)


def nt(a, b):
    return dots(a, b, 1, 1)


def tn(a, b):
    return dots(a, b, 0, 0)


def rms(v, g):
    return v * lax.rsqrt(jnp.mean(v * v, axis=-1, keepdims=True) + eps) * g


def rms_back(v, g, n):
    r = lax.rsqrt(jnp.mean(v * v, axis=-1, keepdims=True) + eps)
    ng = n * g
    return r * ng - v * (r * r * r) * jnp.mean(ng * v, axis=-1, keepdims=True), n * v * r


def gelu_parts(a):
    c = math.sqrt(2 / math.pi)
    t = jnp.tanh(c * (a + 0.044715 * a * a * a))
    half = 0.5 * (1 + t)
    return half * a, half + 0.5 * a * (1 - t * t) * c * (1 + 3 * 0.044715 * a * a)


def place():
    return lax.axis_index("mp"), lax.axis_index("dp"), lax.axis_index("rep")


def peer(k):
    m, z, r = place()
    return (m ^ k, z, r)


def partner():
    m, z, r = place()
    return (m, z, 1 - r)


def greet(core):
    barrier = pltpu.get_barrier_semaphore()
    for k in range(1, WAYS):
        pl.semaphore_signal(barrier, inc=1, device_id=peer(k), device_id_type=MESH)
    if core:
        pl.semaphore_signal(barrier, inc=1, device_id=partner(), device_id_type=MESH)
    pl.semaphore_wait(barrier, WAYS - 1 + core)


def send(src, dst, sems, at, to):
    return pltpu.make_async_remote_copy(
        src_ref=src, dst_ref=dst, send_sem=sems[0].at[at], recv_sem=sems[1].at[at], device_id=to, device_id_type=MESH
    )


def run_kernel(name, phases, ins, outs, scratch, cid, flops=0):
    names = list(ins) + list(outs) + list(scratch)

    def body(*refs):
        held = types.SimpleNamespace(**dict(zip(names, refs)))
        for phase in phases:
            phase(held)

    got = pl.pallas_call(
        body,
        name=name,
        out_shape=[jax.ShapeDtypeStruct(shape, dtype) for shape, dtype, _ in outs.values()],
        in_specs=[pl.BlockSpec(memory_space=space) for _, space in ins.values()],
        out_specs=[pl.BlockSpec(memory_space=space) for _, _, space in outs.values()],
        scratch_shapes=list(scratch.values()),
        compiler_params=pltpu.CompilerParams(
            collective_id=cid, has_side_effects=True, vmem_limit_bytes=60 * 2**20
        ),
        cost_estimate=pl.CostEstimate(flops=flops, bytes_accessed=flops // 200, transcendentals=0),
    )(*[array for array, _ in ins.values()])
    return dict(zip(outs, got))


V, ANY, SM = pltpu.VMEM, pl.ANY, pltpu.SMEM


def dma(*shape):
    return pltpu.SemaphoreType.DMA(shape)


def start_sends(R):
    m, z, r = place()
    quarter = R.mem.shape[1]
    sh = R.wa.shape[1]
    half = sh // 2
    greet(1)
    own = pltpu.make_async_copy(R.mem.at[m], R.memf.at[pl.ds(m * quarter, quarter)], R.l_sem.at[0])
    own.start()
    mine = pltpu.make_async_copy(R.wa, R.waf.at[:, pl.ds(m * sh, sh)], R.l_sem.at[1])
    mine.start()
    R.local = [own, mine]
    R.mem_copies, R.wa_copies, R.fw_copies, R.cot_copies = {}, {}, {}, {}
    rows = pl.ds(m * quarter, quarter)
    for k in range(1, WAYS):
        copy = send(R.mem.at[m ^ k], R.memf.at[rows], (R.mem_s, R.mem_r), k, peer(k))
        copy.start()
        R.mem_copies[k] = copy
    rows = pl.ds(m * sh + r * half, half)
    for part, (lo, n) in enumerate(((0, 2), (2, 3))):
        for k in range(1, WAYS):
            copy = send(
                R.wa.at[pl.ds(lo, n), pl.ds(r * half, half)],
                R.waf.at[pl.ds(lo, n), rows],
                (R.wa_s, R.wa_r),
                part * WAYS + k,
                peer(k),
            )
            copy.start()
            R.wa_copies[part, k] = copy


def send_cot(R):
    m, z, r = place()
    tc = R.cot.shape[1]
    rows = pl.ds(m * tc, tc)
    own = pltpu.make_async_copy(R.cot, R.upall.at[:, rows], R.l_sem.at[2])
    own.start()
    R.local.append(own)
    for k in range(1, WAYS):
        copy = send(R.cot, R.upall.at[:, rows], (R.cot_s, R.cot_r), k, peer(k))
        copy.start()
        R.cot_copies[k] = copy


def forward(R, part):
    m, z, r = place()
    sh = R.wa.shape[1]
    half = sh // 2
    lo, n = ((0, 2), (2, 3))[part]
    for k in range(1, WAYS):
        R.wa_copies[part, k].wait_recv()
        view = R.waf.at[pl.ds(lo, n), pl.ds((m ^ k) * sh + r * half, half)]
        copy = send(view, view, (R.fw_s, R.fw_r), part * WAYS + k, partner())
        copy.start()
        R.fw_copies[part, k] = copy


def self_allowed(R, s):
    T = R.st.shape[1]
    j = lax.broadcasted_iota(jnp.int32, (T, T), 0)
    i = lax.broadcasted_iota(jnp.int32, (T, T), 1)
    return (j == i) | ((j < i) & (R.mask[s] != 0))


def toeplitz(R, h):
    T = R.st.shape[1]
    rows = jnp.broadcast_to(R.vec[h], (T, T))
    return pltpu.roll(rows, 0, 1, stride=1, stride_axis=0)


def self_forward(R):
    m, z, r = place()
    _, T, D = R.st.shape
    HW = R.ws.shape[0] // 3
    heads = R.vec.shape[0]
    hd = HW // heads
    for h in range(heads):
        R.et[h] = toeplitz(R, h)
    R.att_copies = {}

    def one(s):
        normed = rms(R.st[s].astype(F32), R.g_self[...]).astype(BF)
        R.qs[s] = nt(R.ws[0:HW], normed).astype(BF)
        R.ks[s] = nt(normed, R.ws[HW : 2 * HW]).astype(BF)
        R.vs[s] = nt(R.ws[2 * HW : 3 * HW], normed).astype(BF)
        allowed = self_allowed(R, s)
        for h in range(heads):
            rows = slice(h * hd, (h + 1) * hd)
            parts = [R.qs[s, rows] if g == h else jnp.zeros((hd, T), BF) for g in range(heads)]
            scores = nn(R.ks[s], jnp.concatenate(parts, axis=0)) + R.et[h]
            scores = jnp.where(allowed, scores, NEG)
            top = jnp.max(scores, axis=0, keepdims=True)
            weights = jnp.exp(scores - top)
            total = jnp.sum(weights, axis=0, keepdims=True)
            mix = (weights * (1 / total)).astype(BF)
            R.atp[s, rows] = nn(R.vs[s, rows], mix).astype(BF)
            R.lse_s[s, h] = top + jnp.log(total)

    def step(k, carry):
        s = m ^ k
        one(s)
        send(R.atp.at[s], R.att.at[pl.ds(m * HW, HW)], (R.att_s, R.att_r), k, (s, z, r)).start()
        return carry

    lax.fori_loop(1, WAYS, step, 0)
    one(m)
    R.att[pl.ds(pl.multiple_of(m * HW, HW), HW)] = R.atp[m]


def wait_att(R):
    m, z, r = place()
    HW = R.ws.shape[0] // 3
    for k in range(1, WAYS):
        send(R.atp.at[m ^ k], R.att.at[pl.ds(m * HW, HW)], (R.att_s, R.att_r), k, peer(k)).wait()


def cross_kv(R):
    for copy in R.local:
        copy.wait()
    for copy in R.mem_copies.values():
        copy.wait()
    for k in range(1, WAYS):
        R.wa_copies[0, k].wait_send()
        R.fw_copies[0, k].wait()
    M = R.memf.shape[0]
    step = 256

    def rows(i, carry):
        at = pl.ds(pl.multiple_of(i * step, step), step)
        block = R.memf[at]
        k = nt(block, R.waf[CK]).astype(BF)
        R.kc[at] = k
        v = nt(block, R.waf[CV]).astype(BF)
        R.vc[at] = v
        R.kct[:, at] = k.T
        R.vct[:, at] = v.T
        return carry

    lax.fori_loop(0, M // step, rows, 0)


def after_self(R):
    m, z, r = place()
    for k in range(1, WAYS):
        R.wa_copies[1, k].wait_send()
        R.fw_copies[1, k].wait()
    first = R.st[m].astype(F32) + tn(R.att[...], R.waf[SO])
    R.first[...] = first
    normed = rms(first, R.g_cross[...]).astype(BF)
    R.qc[...] = nt(R.waf[CQ], normed).astype(BF)


def padded_head(ref, p, a, hd):
    T = ref.shape[1]
    rows = ref[pl.ds(pl.multiple_of(p * 2 * hd + a * hd, hd), hd)]
    zero = jnp.zeros((hd, T), BF)
    return jnp.concatenate([rows, zero] if a == 0 else [zero, rows], axis=0)


def live_slots(R):
    m, z, r = place()
    M, T = R.memf.shape[0], R.qc.shape[1]
    return lax.broadcasted_iota(jnp.int32, (M, T), 0) < R.lens[m]


def cross_forward(R):
    hd = R.qs.shape[1] // R.vec.shape[0]
    heads = R.qc.shape[0] // hd

    def pair(p, carry):
        lanes = pl.ds(pl.multiple_of(p * 2 * hd, 2 * hd), 2 * hd)
        for a in range(2):
            rows = pl.ds(pl.multiple_of(p * 2 * hd + a * hd, hd), hd)
            scores = nn(R.kc[:, lanes], padded_head(R.qc, p, a, hd))
            scores = jnp.where(live_slots(R), scores, NEG)
            top = jnp.max(scores, axis=0, keepdims=True)
            weights = jnp.exp(scores - top)
            total = jnp.sum(weights, axis=0, keepdims=True)
            mixed = nn(R.vct[rows], weights.astype(BF)) * (1 / total)
            R.attc[rows] = mixed.astype(BF)
            R.lse_c[2 * p + a] = top + jnp.log(total)
        return carry

    lax.fori_loop(0, heads // 2, pair, 0)


def second_part(R):
    m, z, r = place()
    second = R.first[...] + tn(R.attc[...], R.waf[CO])
    R.second[...] = second
    R.nall[m] = rms(second, R.g_ffn[...]).astype(BF)
    copies = [send(R.nall.at[m], R.nall.at[m], (R.nf_s, R.nf_r), k, peer(k)) for k in range(1, WAYS)]
    for copy in copies:
        copy.start()
    for copy in list(R.cot_copies.values()) + copies:
        copy.wait()


def first_phase(R):
    start_sends(R)
    send_cot(R)
    self_forward(R)
    forward(R, 0)
    cross_kv(R)
    forward(R, 1)
    wait_att(R)
    after_self(R)
    cross_forward(R)
    second_part(R)


def per_device(states, memory, target_mask, memory_length, norm_self, self_query, self_key, self_value, self_out,
               bias_table, norm_cross, cross_query, cross_key, cross_value, cross_out, norm_ffn, ffn_gate, ffn_up,
               ffn_down, cotangent):
    me = lax.axis_index("mp")
    ways = WAYS
    T = states.shape[0]
    D = states.shape[2]
    HW = self_query.shape[1]
    HC = bias_table.shape[1]
    hd = HW // HC
    M = memory.shape[0] * ways
    st = jnp.transpose(states, (1, 0, 2))
    mem = jnp.transpose(memory, (1, 0, 2))
    cot = jnp.transpose(cotangent, (1, 0, 2))
    wq, wk, wv = self_query.T, self_key.T, self_value.T
    ws = jnp.concatenate([wq, wk, wv], axis=0)
    wa = jnp.stack([cross_key.T, cross_value.T, self_out, cross_query.T, cross_out])
    pos = jnp.arange(T, dtype=jnp.int32)
    vec = jnp.take(bias_table, bucket_of(pos), axis=0).T[:, None]
    ins = dict(
        st=(st, V), mem=(mem, ANY), ws=(ws, V), wa=(wa, ANY), mask=(target_mask[:, :, None], V), vec=(vec, V),
        lens=(memory_length, SM), g_self=(norm_self[None], V), g_cross=(norm_cross[None], V), g_ffn=(norm_ffn[None], V),
        cot=(cot, ANY),
    )
    heads = D // hd
    outs = dict(
        att=((D, T), BF, V), qs=((ways, HW, T), BF, V), ks=((ways, T, HW), BF, V), vs=((ways, HW, T), BF, V),
        lse_s=((ways, HC, 1, T), F32, V), first=((T, D), F32, V), second=((T, D), F32, V), qc=((D, T), BF, V),
        kc=((M, D), BF, V), kct=((D, M), BF, V), vc=((M, D), BF, V), lse_c=((heads, 1, T), F32, V),
        attc=((D, T), BF, V), memf=((M, D), BF, V), waf=((5, D, D), BF, V), nall=((ways, T, D), BF, V),
        upall=((ways, T, D), BF, V),
    )
    scratch = dict(
        vct=V((D, M), BF), et=V((HC, T, T), F32), atp=V((ways, HW, T), BF), l_sem=dma(3), mem_s=dma(4), mem_r=dma(4),
        wa_s=dma(8), wa_r=dma(8), fw_s=dma(8), fw_r=dma(8), att_s=dma(4), att_r=dma(4), nf_s=dma(4), nf_r=dma(4),
        cot_s=dma(4), cot_r=dma(4),
    )
    G = types.SimpleNamespace(**run_kernel("attend", [first_phase], ins, outs, scratch, 0))
    ck, cv, so, cq, co = (G.waf[i] for i in range(5))
    att_s, first, second, att_c, memf, kc, qc, lc = G.att, G.first, G.second, G.attc, G.memf, G.kc, G.qc, G.lse_c
    vc = G.vc.T
    nall, upall = G.nall, G.upall
    QT, K, VT, LSE = G.qs, G.ks, G.vs, G.lse_s
    a2a = lambda x, si, ci: lax.all_to_all(x, "mp", si, ci, tiled=True)
    dist = jnp.maximum(pos[None, :] - pos[:, None], 0)
    ET = jnp.take(vec[:, 0], dist, axis=1)
    ok = (pos[:, None] <= pos[None, :])[None] & ((target_mask[:, :, None] != 0) | (pos[:, None] == pos[None, :])[None])
    normed = rms(st.astype(F32), norm_self).astype(BF)
    nc = rms(first, norm_cross).astype(BF)
    length = lax.dynamic_index_in_dim(memory_length, me, 0, keepdims=False)
    live = (jnp.arange(M, dtype=jnp.int32) < length)[:, None]
    nr = nall.reshape(ways * T, D)
    ur = upall.reshape(ways * T, D)
    g, u = nn(nr, ffn_gate), nn(nr, ffn_up)
    ge, gd = gelu_parts(g)
    hid = (ge * u).astype(BF)
    branch = nn(hid, ffn_down).reshape(ways, T, D)
    hg = nt(ur, ffn_down)
    gg, ug = (hg * u * gd).astype(BF), (hg * ge).astype(BF)
    down_grad = tn(hid, ur)
    gate_grad = tn(nr, gg)
    up_grad = tn(nr, ug)
    ngp = (nt(gg, ffn_gate) + nt(ug, ffn_up)).reshape(ways, T, D).astype(BF)
    branch = branch + jnp.where(jnp.arange(ways)[:, None, None] == me, second[None], 0)
    br = a2a(branch.astype(BF)[None], 2, 0)
    block_out = jnp.transpose(jnp.sum(br.astype(F32), axis=0), (1, 0, 2)).astype(BF)
    ng = jnp.sum(a2a(ngp, 0, 0).astype(F32), axis=0)
    upown = lax.dynamic_index_in_dim(upall, me, 0, keepdims=False).astype(F32)
    back, gain = rms_back(second, norm_ffn, ng)
    ffn_gain = jnp.sum(gain, axis=0)
    sgrad = upown + back
    cup = sgrad.astype(BF)
    co_grad = nn(att_c, cup)
    doT = nt(co, cup).astype(BF)
    dq, dk, dv = [], [], []
    for h in range(heads):
        sl = slice(h * hd, (h + 1) * hd)
        sT = jnp.where(live, nn(kc[:, sl], qc[sl]), NEG)
        p = jnp.exp(sT - lc[h])
        dpT = tn(vc[sl], doT[sl])
        dv.append(nt(doT[sl], p.astype(BF)).astype(BF))
        ds = (p * (dpT - jnp.sum(p * dpT, axis=0, keepdims=True))).astype(BF)
        dq.append(tn(kc[:, sl], ds).astype(BF))
        dk.append(nt(qc[sl], ds).astype(BF))
    dq, dk, dv = (jnp.concatenate(x, 0) for x in (dq, dk, dv))
    cq_grad, ck_grad, cv_grad = nn(dq, nc), nn(dk, memf), nn(dv, memf)
    mg = (tn(dk, ck) + tn(dv, cv)).astype(BF).reshape(ways, M // ways, D)
    memory_grad = jnp.transpose(a2a(mg, 0, 0).astype(F32), (1, 0, 2))
    ng = tn(dq, cq)
    back, gain = rms_back(first, norm_cross, ng)
    cross_gain = jnp.sum(gain, axis=0)
    fgrad = sgrad + back
    sup = fgrad.astype(BF)
    so_grad = nn(att_s, sup)
    doT = nt(so, sup).astype(BF)
    doT = a2a(doT[None], 1, 0)
    ngs = []
    wqg = wkg = wvg = 0
    dsum = [0] * HC
    for s in range(4):
        dq, dk, dv = [], [], []
        for h in range(HC):
            sl = slice(h * hd, (h + 1) * hd)
            sT = nn(K[s][:, sl], QT[s][sl]) + ET[h]
            sT = jnp.where(ok[s], sT, NEG)
            p = jnp.exp(sT - LSE[s][h])
            dpT = tn(VT[s][sl], doT[s][sl])
            dv.append(nt(doT[s][sl], p.astype(BF)).astype(BF))
            ds = (p * (dpT - jnp.sum(p * dpT, axis=0, keepdims=True))).astype(BF)
            dsum[h] = dsum[h] + ds.astype(F32)
            dq.append(tn(K[s][:, sl], ds).astype(BF))
            dk.append(nt(QT[s][sl], ds).astype(BF))
        dq, dk, dv = (jnp.concatenate(x, 0) for x in (dq, dk, dv))
        wqg, wkg, wvg = wqg + nn(dq, normed[s]), wkg + nn(dk, normed[s]), wvg + nn(dv, normed[s])
        ngs.append(tn(dq, wq) + tn(dk, wk) + tn(dv, wv))
    ngs = jnp.stack(ngs).astype(BF)
    ng = jnp.sum(a2a(ngs[None], 2, 0).astype(F32), axis=0)
    fg = a2a(fgrad.astype(BF)[None], 1, 0).astype(F32)
    tc = T // ways
    v = lax.dynamic_slice_in_dim(st, me * tc, tc, 1).astype(F32)
    back, gain = rms_back(v, norm_self, ng)
    self_gain = jnp.sum(gain, axis=(0, 1))
    states_grad = jnp.transpose(fg + back, (1, 0, 2))
    dd = jnp.stack(dsum)
    diag = jnp.stack([jnp.sum(jnp.where((pos[None, :] - pos[:, None] == r)[None], dd, 0), axis=(1, 2)) for r in range(T)])
    onehot = (bucket_of(pos)[:, None] == jnp.arange(bias_table.shape[0])).astype(F32)
    bias_grad = jnp.einsum("rh,rk->kh", diag, onehot, precision=lax.Precision.HIGHEST)
    cross = jnp.stack([so_grad, cq_grad, ck_grad, cv_grad, co_grad]).astype(BF)
    cross = lax.psum_scatter(cross, "mp", scatter_dimension=1, tiled=True)
    cross = lax.psum(cross.astype(F32), ("dp", "rep"))
    wqg, wkg, wvg, down_grad, gate_grad, up_grad, bias_grad = lax.psum((wqg, wkg, wvg, down_grad, gate_grad, up_grad, bias_grad), ("dp", "rep"))
    gains = lax.psum(jnp.stack([self_gain, cross_gain, ffn_gain]), ("mp", "dp", "rep"))
    return (block_out, states_grad, memory_grad, gains[0], wqg.T, wkg.T, wvg.T, cross[0], bias_grad, gains[1],
            cross[1].T, cross[2].T, cross[3].T, cross[4], gains[2], gate_grad, up_grad, down_grad)


def solution(mesh):
    seq = ("dp", "rep")
    col, row, tok = P(None, "mp"), P("mp", None), P("mp", seq, None)
    in_specs = (P(None, seq, None), tok, P(seq, None), P(seq), P(), col, col, col, row, col, P(), col, col, col, row,
                P(), col, col, row, tok)
    out_specs = (tok, tok, tok, P(), col, col, col, row, col, P(), col, col, col, row, P(), col, col, row)
    return jax.shard_map(per_device, mesh=mesh, in_specs=in_specs, out_specs=out_specs, check_vma=False)
```

time: 919 us -> 1170 us (1.27)
  waiting for transfers between devices: 637 us -> 24.3 us
  local copies, waits for them, and re-layouts: 41.5 us -> 533 us
  other arithmetic: 47.4 us -> 173 us
  Pallas kernels: 0 us -> 114 us
  blocking collectives: 54.4 us -> 157 us
  starting transfers between devices: 1.42 us -> 36.9 us
    psum x5 -> x1, waiting for transfers between devices: 539 us -> 17.1 us  [per_device(): lax.psum((wqg, wkg, wvg, down_grad, gate_grad, up_grad, bias_grad), ('dp'...]
    another operation x0 -> x262, local copies, waits for them, and re-layouts: none -> 235 us  [the longest x257 231 us: per_device(): jnp.stack([jnp.sum(jnp.where((pos[None, :] - pos[:, None] == r)[None], dd...]
    gather x0 -> x4, local copies, waits for them, and re-layouts: none -> 235 us  [the longest x2 234 us: per_device(): ET = jnp.take(vec[:, 0], dist, axis=1)]
    pallas_call x0 -> x1, Pallas kernels: none -> 114 us  [run_kernel(): pl.pallas_call(body, name=name, out_shape=[jax.ShapeDtypeStruct(shape, dt...]
    psum x2, blocking collectives: 54.4 us -> 157 us  [the longest x1 114 us: per_device(): cross = lax.psum(cross.astype(F32), ('dp', 'rep'))]
    all_gather x2 -> x0, waiting for transfers between devices: 91.7 us -> none  [the longest x1 68 us: per_device(): memory_full = lax.all_gather(memory, 'mp', axis=0, tiled=True)]
    eq x1 -> x130, other arithmetic: 0.69 us -> 88.4 us  [the longest x128 87.6 us: per_device(): pos[None, :] - pos[:, None] == r]
    all_to_all x0 -> x6, starting transfers between devices: none -> 36.7 us  [per_device(): a2a = lambda x, si, ci: lax.all_to_all(x, 'mp', si, ci, tiled=True)]
  transfers between devices with their start and end apart: 10 -> 8, of which waited for: 8 -> 2; matrix products, arithmetic and copies ran while one was open for 11% -> 63% of each run, Pallas kernels for 0% -> 0%
where the time goes in v1:
time: 1170 us; the launch traced here: 1160 us
  local copies, waits for them, and re-layouts  533 us (46%)
  other arithmetic  173 us (15%)
  blocking collectives  157 us (13%)
  Pallas kernels  114 us (10%)
  matrix products  103 us (9%)
  starting transfers between devices  36.9 us (3%)
  waiting for transfers between devices  24.3 us (2%)
  between operations  21.4 us (2%)
    gather x2, local copies, waits for them, and re-layouts, per_device(): ET = jnp.take(vec[:, 0], dist, axis=1)  234 us
    another operation x257, local copies, waits for them, and re-layouts, per_device(): jnp.stack([jnp.sum(jnp.where((pos[None, :] - pos[:, None] == r)[None], dd...  231 us
    psum x1, blocking collectives, per_device(): cross = lax.psum(cross.astype(F32), ('dp', 'rep'))  114 us
    pallas_call x1, Pallas kernels, run_kernel(): pl.pallas_call(body, name=name, out_shape=[jax.ShapeDtypeStruct(shape, dt...  114 us
    dot_general x163, matrix products, dots(): lax.dot_general(a, b, (((ca,), (cb,)), ((), ())), preferred_element_type=...  103 us
    eq x128, other arithmetic, per_device(): pos[None, :] - pos[:, None] == r  87.6 us
    reduce_sum x32, other arithmetic, per_device(): jnp.sum(jnp.where((pos[None, :] - pos[:, None] == r)[None], dd, 0), axis=...  48.3 us
    unnamed x931, local copies, waits for them, and re-layouts  47.6 us
  transfers between devices with their start and end apart: 8, of which 2 were waited for; matrix products, arithmetic and copies ran while one was open for 63% of the time, Pallas kernels for 0%

profile of v1, /device:TPU:0, one launch (start us, length us, event | category | flops | bytes accessed | tf_op | source)
XLA Modules:
  0.0 1162.6 jit_solution(15822819886363631545)
XLA Ops:
  22.4 3.9 fusion.671
  27.3 113.7 %attend.1 = (bf16[768,256]{1,0:T(8,128)(2,1)}, bf16[4,192,256]{2,1,0:T(8,128)(2,1)}, bf16[4,256,192]{2,1,0:T(8,128)(2,1)}, bf16[4,192,256]{2,1,0:T(8,128)(2,1)},...) custom-call(bf16[4,256,768]{2,1,0:T(8,128)(2,1)} %get-tuple-element., ...), custom_call_target="tpu_custom_call" | custom-call | tf_op jit(solution)/shard_map/attend/pallas_call | solution.py:97
  141.0 2.5 fusion.676
  144.9 3.1 multiply_convert_fusion
  151.8 14.9 %all-to-all-start.1 = ((bf16[4,256,768]{2,1,0:T(8,128)(2,1)}), bf16[4,256,768]{2,1,0:T(8,128)(2,1)}, u32[]{:S(2)}, u32[]{:S(2)}) async-start(bf16[4,256,768]{2,1,0:T(8,128)(2,1)} %bitcast.801), calls=%async_computation.1 | async-start | bytes 3145728 | tf_op jit(solution)/shard_map/all_to_all | solution.py:373
  256.9 2.2 fusion.680
  271.3 215.5 %gather_fusion.1 = f32[65536,3]{1,0:T(8,128)} fusion(f32[3,256]{0,1:T(8,128)S(1)} %copy.626, s32[65536]{0:T(1024)S(1)} %copy-done.46), kind=kCustom, calls=%fused_computation.1 | custom fusion | bytes 1835008 | tf_op jit(solution)/shard_map/jit(_take)/gather | solution.py:375
  486.8 18.8 %copy.899 = f32[256,256,3]{1,0,2:T(8,128)S(1)} copy(f32[256,256,3]{2,1,0:T(8,128)} %bitcast.796) | data formatting | bytes 1572864 | tf_op jit(solution)/shard_map/jit(_take)/gather | solution.py:375
  507.4 3.6 fusion.681
  512.2 3.6 fusion.3
  515.8 4.7 all-to-all-start
  545.5 2.3 reduce_sum.2666
  578.8 3.8 reduce.14
  584.4 4.1 all-to-all-start.3
  590.4 3.8 reduce.13
  596.0 4.9 fusion.59
  604.0 2.4 fusion.13
  606.4 2.4 fusion.15
  611.8 4.8 add_convert_fusion
  616.6 4.2 all-to-all-start.2
  620.8 2.6 reshape.3024
  693.7 4.3 all-to-all-start.5
  699.6 2.4 copy.638
  708.6 7.2 all-to-all-done.5
  715.8 4.4 all-to-all-start.4
  721.6 2.3 reshape.3022
  960.0 3.7 copy.898
  963.6 2.4 convert_reduce_fusion
  968.2 42.4 %psum.63 = f32[3,768]{1,0:T(4,128)S(1)} all-reduce(f32[3,768]{1,0:T(4,128)S(1)} %pad_maximum_fusion.39), channel_id=1, replica_groups=mesh['mp'=4,'dp'=4,'rep'=2] {'mp','dp','rep'}, use_global_device_ids=true, to_apply=%region_37.38 | all-reduce | flops 2304 | bytes 18432 | tf_op jit(solution)/shard_map/psum | solution.py:461
  1011.2 114.4 %all-reduce.6 = (f32[5,192,768]{2,1,0:T(8,128)}, f32[32,3]{0,1:T(4,128)}) all-reduce(bf16[5,192,768]{2,1,0:T(8,128)(2,1)} %reduce-scatter.2.cloned.1.call-done, f32[32,3]{0,1:T(4,128)S(1)} %fusion.485), channel_id=1, replica_groups=mesh['mp'=4,'dp'=4,'rep'=2] {'dp','rep'}, use_global_device_ids=true, to_apply=%region_43.44 | all-reduce | flops 737376 | bytes 4424448 | tf_op jit(solution)/shard_map/psum | solution.py:459
  1125.6 3.5 slice_bitcast_fusion
  1129.0 17.1 %all-reduce.5.cloned.1.call-done = (f32[768,192]{0,1:T(8,128)}, f32[768,192]{0,1:T(8,128)}, f32[768,192]{0,1:T(8,128)}, f32[768,512]{1,0:T(8,128)}, f32[768,512]{1,0:T(8,128)}, /*index=5*/f32[512,768]{1,0:T(8,128)}) async-done(((f32[768,192]{0,1:T(8,128)}, f32[768,192]{0,1:T(8,128)}, f32[768,192]{0,1:T(8,128)}, f32[768,512]{1,0:T(8,128)}, f32[768,512]{1,0:T(8,128)}, /*index=5*/f32[512,768]{1,0:T(8,128)}), ...) | async-done | bytes 6488080 | tf_op jit(solution)/shard_map/psum | solution.py:460
  (1582 shorter events, 515.3 us)
Async XLA Ops:
  8.0 136.5 %copy-start = (bf16[512,768]{1,0:T(8,128)(2,1)S(1)}, bf16[512,768]{1,0:T(8,128)(2,1)}, u32[]{:S(2)}) copy-start(bf16[512,768]{1,0:T(8,128)(2,1)} %param.40) | copy-start | bytes 2359300
  27.3 113.7 %copy-start.48 = (bf16[768,512]{1,0:T(8,128)(2,1)S(1)}, bf16[768,512]{1,0:T(8,128)(2,1)}, u32[]{:S(2)}) copy-start(bf16[768,512]{1,0:T(8,128)(2,1)} %param.39) | copy-start | bytes 2359300
  151.8 364.0 %all-to-all-start.1 = ((bf16[4,256,768]{2,1,0:T(8,128)(2,1)}), bf16[4,256,768]{2,1,0:T(8,128)(2,1)}, u32[]{:S(2)}, u32[]{:S(2)}) async-start(bf16[4,256,768]{2,1,0:T(8,128)(2,1)} %bitcast.801), calls=%async_computation.1 | async-start | bytes 3145728 | tf_op jit(solution)/shard_map/all_to_all | solution.py:373
  241.2 15.7 %copy-start.45 = (bf16[1024,512]{1,0:T(8,128)(2,1)S(1)}, bf16[1024,512]{1,0:T(8,128)(2,1)}, u32[]{:S(2)}) copy-start(bf16[1024,512]{1,0:T(8,128)(2,1)} %copy-done.44) | copy-start | bytes 3145732
  241.2 15.7 %copy-start.451 = (bf16[4,256,768]{2,1,0:T(8,128)(2,1)S(1)}, bf16[4,256,768]{2,1,0:T(8,128)(2,1)}, u32[]{:S(2)}) copy-start(bf16[4,256,768]{2,1,0:T(8,128)(2,1)} %get-tuple-element.34) | copy-start | bytes 4718596
  486.8 18.8 %copy-start.336 = (pred[256,256]{1,0:T(8,128)(4,1)S(1)}, pred[256,256]{1,0:T(8,128)(4,1)}, u32[]{:S(2)}) copy-start(pred[256,256]{1,0:T(8,128)(4,1)} %maximum_compare_fusion) | copy-start | bytes 196612
  515.8 29.8 %all-to-all-start = ((bf16[1,4,256,768]{3,1,0,2:T(4,128)(2,1)}), bf16[1,4,256,768]{3,1,0,2:T(4,128)(2,1)}, u32[]{:S(2)}, u32[]{:S(2)}) async-start(bf16[1,4,256,768]{3,1,0,2:T(4,128)(2,1)} %fusion.3), calls=%async_computation | async-start | bytes 3145728 | tf_op jit(solution)/shard_map/all_to_all | solution.py:373
  526.0 18.2 %copy-start.42 = (bf16[768,256]{1,0:T(8,128)(2,1)}, bf16[768,256]{1,0:T(8,128)(2,1)S(1)}, u32[]{:S(2)}) copy-start(bf16[768,256]{1,0:T(8,128)(2,1)S(1)} %convolution_convert_fusion.6) | copy-start | bytes 1179652
  584.4 32.2 %all-to-all-start.3 = ((bf16[4,2,24576]{2,1,0:T(2,128)(2,1)}), bf16[4,2,24576]{2,1,0:T(2,128)(2,1)}, u32[]{:S(2)}, u32[]{:S(2)}) async-start(bf16[4,2,24576]{2,1,0:T(2,128)(2,1)} %reshape.3023), calls=%async_computation.3 | async-start | bytes 786432 | tf_op jit(solution)/shard_map/all_to_all | solution.py:373
  588.6 422.6 %reduce-scatter.2.cloned.1.call-start = ((), (), s32[]{:S(2)}) async-start(), calls=%async_computation.7 | async-start | bytes 7372800 | tf_op jit(solution)/shard_map/reduce_scatter | solution.py:458
  616.6 77.0 %all-to-all-start.2 = ((bf16[4,2,24576]{2,1,0:T(2,128)(2,1)}), bf16[4,2,24576]{2,1,0:T(2,128)(2,1)}, u32[]{:S(2)}, u32[]{:S(2)}) async-start(bf16[4,2,24576]{2,1,0:T(2,128)(2,1)} %reshape.3021), calls=%async_computation.2 | async-start | bytes 786432 | tf_op jit(solution)/shard_map/all_to_all | solution.py:373
  625.8 65.1 %copy-start.71 = (bf16[64,256]{1,0:T(8,128)(2,1)}, bf16[64,256]{1,0:T(8,128)(2,1)S(1)}, u32[]{:S(2)}) copy-start(bf16[64,256]{1,0:T(8,128)(2,1)S(1)} %convolution_convert_fusion.49) | copy-start | bytes 98308
  626.3 16.8 %copy-start.59 = (bf16[64,256]{1,0:T(8,128)(2,1)}, bf16[64,256]{1,0:T(8,128)(2,1)S(1)}, u32[]{:S(2)}) copy-start(bf16[64,256]{1,0:T(8,128)(2,1)S(1)} %convolution_convert_fusion.40) | copy-start | bytes 98308
  626.7 15.3 %copy-start.61 = (bf16[64,256]{1,0:T(8,128)(2,1)}, bf16[64,256]{1,0:T(8,128)(2,1)S(1)}, u32[]{:S(2)}) copy-start(bf16[64,256]{1,0:T(8,128)(2,1)S(1)} %convolution_convert_fusion.31) | copy-start | bytes 98308
  629.9 61.1 %copy-start.73 = (bf16[64,256]{1,0:T(8,128)(2,1)}, bf16[64,256]{1,0:T(8,128)(2,1)S(1)}, u32[]{:S(2)}) copy-start(bf16[64,256]{1,0:T(8,128)(2,1)S(1)} %convolution_convert_fusion.50) | copy-start | bytes 98308
  630.4 12.7 %copy-start.63 = (bf16[64,256]{1,0:T(8,128)(2,1)}, bf16[64,256]{1,0:T(8,128)(2,1)S(1)}, u32[]{:S(2)}) copy-start(bf16[64,256]{1,0:T(8,128)(2,1)S(1)} %convolution_convert_fusion.41) | copy-start | bytes 98308
  630.9 11.1 copy-start.65
  633.1 57.9 %copy-start.75 = (bf16[64,256]{1,0:T(8,128)(2,1)}, bf16[64,256]{1,0:T(8,128)(2,1)S(1)}, u32[]{:S(2)}) copy-start(bf16[64,256]{1,0:T(8,128)(2,1)S(1)} %convolution_convert_fusion.51) | copy-start | bytes 98308
  633.5 9.6 copy-start.67
  693.7 22.2 %all-to-all-start.5 = ((bf16[4,256,768]{2,1,0:T(8,128)(2,1)}), bf16[4,256,768]{2,1,0:T(8,128)(2,1)}, u32[]{:S(2)}, u32[]{:S(2)}) async-start(bf16[4,256,768]{2,1,0:T(8,128)(2,1)} %bitcast.820), calls=%async_computation.5 | async-start | bytes 3145728 | tf_op jit(solution)/shard_map/all_to_all | solution.py:373
  708.6 11.7 %copy-start.72 = (bf16[64,256]{1,0:T(8,128)(2,1)S(1)}, bf16[64,256]{1,0:T(8,128)(2,1)}, u32[]{:S(2)}) copy-start(bf16[64,256]{1,0:T(8,128)(2,1)} %copy-done.71) | copy-start | bytes 98308
  708.6 11.7 %copy-start.74 = (bf16[64,256]{1,0:T(8,128)(2,1)S(1)}, bf16[64,256]{1,0:T(8,128)(2,1)}, u32[]{:S(2)}) copy-start(bf16[64,256]{1,0:T(8,128)(2,1)} %copy-done.73) | copy-start | bytes 98308
  708.6 11.7 %copy-start.76 = (bf16[64,256]{1,0:T(8,128)(2,1)S(1)}, bf16[64,256]{1,0:T(8,128)(2,1)}, u32[]{:S(2)}) copy-start(bf16[64,256]{1,0:T(8,128)(2,1)} %copy-done.75) | copy-start | bytes 98308
  715.8 247.8 %all-to-all-start.4 = ((bf16[1,4,256,768]{3,1,0,2:T(4,128)(2,1)}), bf16[1,4,256,768]{3,1,0,2:T(4,128)(2,1)}, u32[]{:S(2)}, u32[]{:S(2)}) async-start(bf16[1,4,256,768]{3,1,0,2:T(4,128)(2,1)} %copy.638), calls=%async_computation.4 | async-start | bytes 3145728 | tf_op jit(solution)/shard_map/all_to_all | solution.py:373
  720.2 425.9 %all-reduce.5.cloned.1.call-start = ((), (), s32[]{:S(2)}) async-start(), calls=%async_computation.8 | async-start | bytes 12976128 | tf_op jit(solution)/shard_map/psum | solution.py:460
  723.9 229.4 %copy-start.60 = (bf16[64,256]{1,0:T(8,128)(2,1)S(1)}, bf16[64,256]{1,0:T(8,128)(2,1)}, u32[]{:S(2)}) copy-start(bf16[64,256]{1,0:T(8,128)(2,1)} %copy-done.59) | copy-start | bytes 98308
  723.9 229.4 %copy-start.64 = (bf16[64,256]{1,0:T(8,128)(2,1)S(1)}, bf16[64,256]{1,0:T(8,128)(2,1)}, u32[]{:S(2)}) copy-start(bf16[64,256]{1,0:T(8,128)(2,1)} %copy-done.63) | copy-start | bytes 98308
  723.9 229.4 %copy-start.68 = (bf16[64,256]{1,0:T(8,128)(2,1)S(1)}, bf16[64,256]{1,0:T(8,128)(2,1)}, u32[]{:S(2)}) copy-start(bf16[64,256]{1,0:T(8,128)(2,1)} %copy-done.67) | copy-start | bytes 98308
  724.0 229.4 %copy-start.31 = (f32[192,768]{1,0:T(8,128)S(1)}, f32[192,768]{1,0:T(8,128)}, u32[]{:S(2)}) copy-start(f32[192,768]{1,0:T(8,128)} %convolution_add_fusion.10) | copy-start | bytes 1769476
  726.5 227.1 %copy-start.62 = (bf16[64,256]{1,0:T(8,128)(2,1)S(1)}, bf16[64,256]{1,0:T(8,128)(2,1)}, u32[]{:S(2)}) copy-start(bf16[64,256]{1,0:T(8,128)(2,1)} %copy-done.61) | copy-start | bytes 98308
  726.5 227.1 %copy-start.66 = (bf16[64,256]{1,0:T(8,128)(2,1)S(1)}, bf16[64,256]{1,0:T(8,128)(2,1)}, u32[]{:S(2)}) copy-start(bf16[64,256]{1,0:T(8,128)(2,1)} %copy-done.65) | copy-start | bytes 98308
  726.5 227.1 %copy-start.70 = (bf16[64,256]{1,0:T(8,128)(2,1)S(1)}, bf16[64,256]{1,0:T(8,128)(2,1)}, u32[]{:S(2)}) copy-start(bf16[64,256]{1,0:T(8,128)(2,1)} %copy-done.69) | copy-start | bytes 98308
  (429 other events, 1218.2 us)
Sparse Core Ops, SparseCore 0:
  610.5 72.8 reduce-scatter.1
Sparse Core Ops, SparseCore 1:
  955.1 190.9 all-reduce.4
